TPU v7x, 256 devices: a whole 4x4x8 slice. The times are simulated.
256 devices in a mesh: row: 8 (over x, core), col: 32 (over z, y).
Axes of the slice: x: 4, y: 4, z: 8, core: 2. Of those that a mesh axis runs over, the one named last changes fastest.
Arguments:
- points: float32 [65536, 32], P(('row', 'col')), may hold values from -6 to 6
- inv_length: float32 [32], replicated, may hold values from 0.1 to 0.3
- solution: float32 [65536, 8], P(('row', 'col')), may hold values from -6 to 6
- residual: float32 [65536, 8], P(('row', 'col')), may hold values from -6 to 6
- direction: float32 [65536, 8], P(('row', 'col')), may hold values from -6 to 6
Outputs:
- new_solution: float32 [65536, 8], P(('row', 'col'))
- new_residual: float32 [65536, 8], P(('row', 'col'))
- new_direction: float32 [65536, 8], P(('row', 'col'))
All inputs are finite; a program needn't handle non-finite values.
Results may differ from a plain program's by a relative error of at most 0.00011.
Values sent between devices are 32-bit elements; how exact they have to be, the bound alone decides.
A program may use at most 192 MiB of HBM per device.

v0:
```python
import math

import jax
import jax.numpy as jnp
from jax import lax
from jax.sharding import PartitionSpec as P

root_five = math.sqrt(5.0)
noise_level = 0.1


def kernel_tile(row_s, row_q, col_s, col_q):
    cross = jnp.dot(
        row_s, col_s.T, precision=lax.Precision.HIGHEST, preferred_element_type=jnp.float32
    )
    dist_sq = jnp.maximum(row_q[:, None] + col_q[None, :] - 2.0 * cross, 0.0)
    scaled_r = root_five * jnp.sqrt(dist_sq)
    return (1.0 + scaled_r + scaled_r * scaled_r / 3.0) * jnp.exp(-scaled_r)


def kernel_product(row_s, row_q, col_s, col_q, col_v):
    kernel = kernel_tile(row_s, row_q, col_s, col_q)
    return jnp.dot(
        kernel, col_v, precision=lax.Precision.HIGHEST, preferred_element_type=jnp.float32
    )


def fold_columns(totals, row_s, row_q, col_points, col_dir, inv_length, widest):
    col_s = col_points * inv_length
    col_q = jnp.sum(col_s * col_s, axis=1)
    count = col_s.shape[0]
    width = math.gcd(count, widest)
    turns = count // width

    def advance(block_index, accum):
        anchor = block_index * width
        block_s = lax.dynamic_slice_in_dim(col_s, anchor, width, 0)
        block_q = lax.dynamic_slice_in_dim(col_q, anchor, width, 0)
        block_v = lax.dynamic_slice_in_dim(col_dir, anchor, width, 0)
        return accum + kernel_product(row_s, row_q, block_s, block_q, block_v)

    return lax.fori_loop(0, turns, advance, totals)


def local(points, inv_length, solution, residual, direction):
    norm_old = lax.psum(jnp.sum(residual * residual, axis=0), ("row", "col"))
    row_points = lax.all_gather(points, "col", axis=0, tiled=True)
    row_s = row_points * inv_length
    row_q = jnp.sum(row_s * row_s, axis=1)
    empty = jnp.zeros((row_s.shape[0], direction.shape[1]), jnp.float32)
    partial_sum = fold_columns(
        empty,
        row_s,
        row_q,
        lax.all_gather(points, "row", axis=0, tiled=True),
        lax.all_gather(direction, "row", axis=0, tiled=True),
        inv_length,
        256,
    )
    image = lax.psum_scatter(partial_sum, "col", scatter_dimension=0, tiled=True)
    image = image + noise_level * direction
    curvature = lax.psum(jnp.sum(direction * image, axis=0), ("row", "col"))
    step_size = norm_old / curvature
    new_solution = solution + step_size * direction
    new_residual = residual - step_size * image
    norm_new = lax.psum(jnp.sum(new_residual * new_residual, axis=0), ("row", "col"))
    new_direction = new_residual + norm_new / norm_old * direction
    return (new_solution, new_residual, new_direction)


def solution(mesh):
    placed = (
        P(("row", "col"), None),
        P(),
        P(("row", "col"), None),
        P(("row", "col"), None),
        P(("row", "col"), None),
    )
    return jax.shard_map(
        local,
        mesh=mesh,
        in_specs=placed,
        out_specs=(P(("row", "col"), None), P(("row", "col"), None), P(("row", "col"), None)),
        check_vma=False,
    )
```

profile of v0, /device:TPU:1, one launch (start us, length us, event | category | flops | bytes accessed | tf_op | source)
XLA Modules:
  0.0 645.5 jit_solution(7975672718994906888)
XLA Ops:
  7.2 0.0 all-gather.2.cloned.1.call-start
  7.2 1.5 copy.8
  8.7 0.0 all-gather.2.cloned.1.call-update
  8.7 0.0 reduce-scatter.2.cloned.1.call-start
  8.8 16.0 %all_gather.11 = f32[2048,8]{0,1:T(8,128)S(1)} all-gather(f32[256,8]{0,1:T(8,128)} %param.11), channel_id=1, replica_groups=mesh['row'=8,'col'=32] {'row'}, dimensions={0}, use_global_device_ids=true | all-gather | bytes 73728 | tf_op jit(solution)/shard_map/all_gather | solution.py:56
  24.8 14.0 %all_gather.10 = f32[2048,32]{1,0:T(8,128)S(1)} all-gather(f32[256,32]{1,0:T(8,128)} %copy.8), channel_id=1, replica_groups=mesh['row'=8,'col'=32] {'row'}, dimensions={0}, use_global_device_ids=true | all-gather | bytes 294912 | tf_op jit(solution)/shard_map/all_gather | solution.py:55
  38.8 1.0 multiply_reduce_fusion.1
  39.8 53.8 %all-gather.2.cloned.1.call-done = f32[8192,32]{1,0:T(8,128)} async-done(((f32[256,32]{1,0:T(8,128)}), f32[8192,32]{1,0:T(8,128)}) %all-gather.2.cloned.1.call-update) | async-done | bytes 1048592 | tf_op jit(solution)/shard_map/all_gather | solution.py:47
  93.6 5.2 multiply_reduce_fusion
  98.8 175.6 %while.14 = (s32[]{:T(128)}, f32[8192,8]{0,1:T(8,128)S(1)}, f32[8192]{0:T(1024)S(1)}, f32[2048]{0:T(1024)S(1)}, f32[2048,32]{1,0:T(8,128)S(1)}, /*index=5*/f32[8...) while((s32[]{:T(128)}, f32[8192,8]{0,1:T(8,128)S(1)}, ...), condition=%wide.region_5.0_spmd.clone, body=%wide.region_4.0_spmd.clone.sunk | while | flops 1029832704 | bytes 18525360 | solution.py:42
  98.8 0.1 dynamic_slice.33
  98.9 13.3 %fusion.30 = f32[8192,256]{0,1:T(8,128)} fusion(f32[8192,32]{1,0:T(8,128)} %get-tuple-element.245, f32[256]{0:T(256)S(1)} %dynamic_slice.33, f32[8192]{0:T(1024)S(1)} %get-tuple-element.242, f32[2048,32]{1,0:T(8,128)S(1)} %get-tuple-element.244, s32[]{:T(128)S(6)} %select_n.11), kind=kOutput, calls=%fused_computation.5.clone.1 | convolution fusion | flops 815792128 | bytes 9602052 | tf_op jit(solution)/shard_map/while/body/eval_jaxpr/dot_general | solution.py:13
  112.2 8.5 %convolution_add_fusion.2 = f32[8192,8]{0,1:T(8,128)S(1)} fusion(f32[8192,256]{0,1:T(8,128)} %fusion.30, f32[8192,8]{0,1:T(8,128)S(1)} %get-tuple-element.230, pred[]{:T(512)S(6)} %compare.3, f32[2048,8]{0,1:T(8,128)S(1)} %get-tuple-element.246, s32[]{:T(128)S(6)} %select_n.11), kind=kOutput, calls=%fused_computation.6.clone.1 | convolution fusion | flops 214040576 | bytes 8921093 | tf_op jit(solution)/shard_map/while/body/eval_jaxpr/dot_general | solution.py:23
  120.7 0.1 dynamic_slice.33
  120.8 13.3 %fusion.30 = f32[8192,256]{0,1:T(8,128)} fusion(f32[8192,32]{1,0:T(8,128)} %get-tuple-element.245, f32[256]{0:T(256)S(1)} %dynamic_slice.33, f32[8192]{0:T(1024)S(1)} %get-tuple-element.242, f32[2048,32]{1,0:T(8,128)S(1)} %get-tuple-element.244, s32[]{:T(128)S(6)} %select_n.11), kind=kOutput, calls=%fused_computation.5.clone.1 | convolution fusion | flops 815792128 | bytes 9602052 | tf_op jit(solution)/shard_map/while/body/eval_jaxpr/dot_general | solution.py:13
  134.2 8.5 %convolution_add_fusion.2 = f32[8192,8]{0,1:T(8,128)S(1)} fusion(f32[8192,256]{0,1:T(8,128)} %fusion.30, f32[8192,8]{0,1:T(8,128)S(1)} %get-tuple-element.230, pred[]{:T(512)S(6)} %compare.3, f32[2048,8]{0,1:T(8,128)S(1)} %get-tuple-element.246, s32[]{:T(128)S(6)} %select_n.11), kind=kOutput, calls=%fused_computation.6.clone.1 | convolution fusion | flops 214040576 | bytes 8921093 | tf_op jit(solution)/shard_map/while/body/eval_jaxpr/dot_general | solution.py:23
  142.7 0.1 dynamic_slice.33
  142.8 13.3 %fusion.30 = f32[8192,256]{0,1:T(8,128)} fusion(f32[8192,32]{1,0:T(8,128)} %get-tuple-element.245, f32[256]{0:T(256)S(1)} %dynamic_slice.33, f32[8192]{0:T(1024)S(1)} %get-tuple-element.242, f32[2048,32]{1,0:T(8,128)S(1)} %get-tuple-element.244, s32[]{:T(128)S(6)} %select_n.11), kind=kOutput, calls=%fused_computation.5.clone.1 | convolution fusion | flops 815792128 | bytes 9602052 | tf_op jit(solution)/shard_map/while/body/eval_jaxpr/dot_general | solution.py:13
  156.1 8.5 %convolution_add_fusion.2 = f32[8192,8]{0,1:T(8,128)S(1)} fusion(f32[8192,256]{0,1:T(8,128)} %fusion.30, f32[8192,8]{0,1:T(8,128)S(1)} %get-tuple-element.230, pred[]{:T(512)S(6)} %compare.3, f32[2048,8]{0,1:T(8,128)S(1)} %get-tuple-element.246, s32[]{:T(128)S(6)} %select_n.11), kind=kOutput, calls=%fused_computation.6.clone.1 | convolution fusion | flops 214040576 | bytes 8921093 | tf_op jit(solution)/shard_map/while/body/eval_jaxpr/dot_general | solution.py:23
  164.6 0.1 dynamic_slice.33
  164.7 13.3 %fusion.30 = f32[8192,256]{0,1:T(8,128)} fusion(f32[8192,32]{1,0:T(8,128)} %get-tuple-element.245, f32[256]{0:T(256)S(1)} %dynamic_slice.33, f32[8192]{0:T(1024)S(1)} %get-tuple-element.242, f32[2048,32]{1,0:T(8,128)S(1)} %get-tuple-element.244, s32[]{:T(128)S(6)} %select_n.11), kind=kOutput, calls=%fused_computation.5.clone.1 | convolution fusion | flops 815792128 | bytes 9602052 | tf_op jit(solution)/shard_map/while/body/eval_jaxpr/dot_general | solution.py:13
  178.0 8.5 %convolution_add_fusion.2 = f32[8192,8]{0,1:T(8,128)S(1)} fusion(f32[8192,256]{0,1:T(8,128)} %fusion.30, f32[8192,8]{0,1:T(8,128)S(1)} %get-tuple-element.230, pred[]{:T(512)S(6)} %compare.3, f32[2048,8]{0,1:T(8,128)S(1)} %get-tuple-element.246, s32[]{:T(128)S(6)} %select_n.11), kind=kOutput, calls=%fused_computation.6.clone.1 | convolution fusion | flops 214040576 | bytes 8921093 | tf_op jit(solution)/shard_map/while/body/eval_jaxpr/dot_general | solution.py:23
  186.6 0.1 dynamic_slice.33
  186.7 13.3 %fusion.30 = f32[8192,256]{0,1:T(8,128)} fusion(f32[8192,32]{1,0:T(8,128)} %get-tuple-element.245, f32[256]{0:T(256)S(1)} %dynamic_slice.33, f32[8192]{0:T(1024)S(1)} %get-tuple-element.242, f32[2048,32]{1,0:T(8,128)S(1)} %get-tuple-element.244, s32[]{:T(128)S(6)} %select_n.11), kind=kOutput, calls=%fused_computation.5.clone.1 | convolution fusion | flops 815792128 | bytes 9602052 | tf_op jit(solution)/shard_map/while/body/eval_jaxpr/dot_general | solution.py:13
  200.0 8.5 %convolution_add_fusion.2 = f32[8192,8]{0,1:T(8,128)S(1)} fusion(f32[8192,256]{0,1:T(8,128)} %fusion.30, f32[8192,8]{0,1:T(8,128)S(1)} %get-tuple-element.230, pred[]{:T(512)S(6)} %compare.3, f32[2048,8]{0,1:T(8,128)S(1)} %get-tuple-element.246, s32[]{:T(128)S(6)} %select_n.11), kind=kOutput, calls=%fused_computation.6.clone.1 | convolution fusion | flops 214040576 | bytes 8921093 | tf_op jit(solution)/shard_map/while/body/eval_jaxpr/dot_general | solution.py:23
  208.5 0.1 dynamic_slice.33
  208.6 13.3 %fusion.30 = f32[8192,256]{0,1:T(8,128)} fusion(f32[8192,32]{1,0:T(8,128)} %get-tuple-element.245, f32[256]{0:T(256)S(1)} %dynamic_slice.33, f32[8192]{0:T(1024)S(1)} %get-tuple-element.242, f32[2048,32]{1,0:T(8,128)S(1)} %get-tuple-element.244, s32[]{:T(128)S(6)} %select_n.11), kind=kOutput, calls=%fused_computation.5.clone.1 | convolution fusion | flops 815792128 | bytes 9602052 | tf_op jit(solution)/shard_map/while/body/eval_jaxpr/dot_general | solution.py:13
  221.9 8.5 %convolution_add_fusion.2 = f32[8192,8]{0,1:T(8,128)S(1)} fusion(f32[8192,256]{0,1:T(8,128)} %fusion.30, f32[8192,8]{0,1:T(8,128)S(1)} %get-tuple-element.230, pred[]{:T(512)S(6)} %compare.3, f32[2048,8]{0,1:T(8,128)S(1)} %get-tuple-element.246, s32[]{:T(128)S(6)} %select_n.11), kind=kOutput, calls=%fused_computation.6.clone.1 | convolution fusion | flops 214040576 | bytes 8921093 | tf_op jit(solution)/shard_map/while/body/eval_jaxpr/dot_general | solution.py:23
  230.5 0.1 dynamic_slice.33
  230.5 13.3 %fusion.30 = f32[8192,256]{0,1:T(8,128)} fusion(f32[8192,32]{1,0:T(8,128)} %get-tuple-element.245, f32[256]{0:T(256)S(1)} %dynamic_slice.33, f32[8192]{0:T(1024)S(1)} %get-tuple-element.242, f32[2048,32]{1,0:T(8,128)S(1)} %get-tuple-element.244, s32[]{:T(128)S(6)} %select_n.11), kind=kOutput, calls=%fused_computation.5.clone.1 | convolution fusion | flops 815792128 | bytes 9602052 | tf_op jit(solution)/shard_map/while/body/eval_jaxpr/dot_general | solution.py:13
  243.9 8.5 %convolution_add_fusion.2 = f32[8192,8]{0,1:T(8,128)S(1)} fusion(f32[8192,256]{0,1:T(8,128)} %fusion.30, f32[8192,8]{0,1:T(8,128)S(1)} %get-tuple-element.230, pred[]{:T(512)S(6)} %compare.3, f32[2048,8]{0,1:T(8,128)S(1)} %get-tuple-element.246, s32[]{:T(128)S(6)} %select_n.11), kind=kOutput, calls=%fused_computation.6.clone.1 | convolution fusion | flops 214040576 | bytes 8921093 | tf_op jit(solution)/shard_map/while/body/eval_jaxpr/dot_general | solution.py:23
  252.4 0.1 dynamic_slice.33
  252.5 13.3 %fusion.30 = f32[8192,256]{0,1:T(8,128)} fusion(f32[8192,32]{1,0:T(8,128)} %get-tuple-element.245, f32[256]{0:T(256)S(1)} %dynamic_slice.33, f32[8192]{0:T(1024)S(1)} %get-tuple-element.242, f32[2048,32]{1,0:T(8,128)S(1)} %get-tuple-element.244, s32[]{:T(128)S(6)} %select_n.11), kind=kOutput, calls=%fused_computation.5.clone.1 | convolution fusion | flops 815792128 | bytes 9602052 | tf_op jit(solution)/shard_map/while/body/eval_jaxpr/dot_general | solution.py:13
  265.8 8.5 %convolution_add_fusion.2 = f32[8192,8]{0,1:T(8,128)S(1)} fusion(f32[8192,256]{0,1:T(8,128)} %fusion.30, f32[8192,8]{0,1:T(8,128)S(1)} %get-tuple-element.230, pred[]{:T(512)S(6)} %compare.3, f32[2048,8]{0,1:T(8,128)S(1)} %get-tuple-element.246, s32[]{:T(128)S(6)} %select_n.11), kind=kOutput, calls=%fused_computation.6.clone.1 | convolution fusion | flops 214040576 | bytes 8921093 | tf_op jit(solution)/shard_map/while/body/eval_jaxpr/dot_general | solution.py:23
  274.3 0.0 copy-start
  274.4 0.7 copy-done
  275.0 0.0 reduce-scatter.2.cloned.1.call-update
  275.1 0.0 copy-done.3
  275.1 0.1 multiply_reduce_fusion.4
  275.2 207.4 %reduce-scatter.2.cloned.1.call-done = f32[256,8]{0,1:T(8,128)} async-done(((f32[8192,8]{0,1:T(8,128)}), f32[256,8]{0,1:T(8,128)}) %reduce-scatter.2.cloned.1.call-update) | async-done | bytes 8208 | tf_op jit(solution)/shard_map/reduce_scatter | solution.py:60
  482.6 0.0 copy-done.1
  482.6 0.8 multiply_reduce_fusion.3
  483.4 79.8 %all-reduce = (f32[8]{0:T(128)S(1)}, f32[8]{0:T(128)S(1)}) all-reduce(f32[8]{0:T(128)S(1)} %multiply_reduce_fusion.4, f32[8]{0:T(128)S(1)} %multiply_reduce_fusion.3), channel_id=1, replica_groups=mesh['row'=8,'col'=32] {'row','col'}, use_global_device_ids=true, to_apply=%region_1.0 | all-reduce | flops 16 | bytes 128 | tf_op jit(solution)/shard_map/psum | solution.py:46
  563.2 0.0 copy-done.4
  563.2 1.5 multiply_reduce_fusion.2
  564.7 73.3 %psum.23 = f32[8]{0:T(128)S(1)} all-reduce(f32[8]{0:T(128)S(1)} %get-tuple-element.168), channel_id=1, replica_groups=mesh['row'=8,'col'=32] {'row','col'}, use_global_device_ids=true, to_apply=%region_10.0 | all-reduce | flops 8 | bytes 64 | tf_op jit(solution)/shard_map/psum | solution.py:66
  638.0 0.7 multiply_add_fusion
  638.7 0.0 copy-done.2
  (7 shorter events, 0.0 us)
Async XLA Ops:
  7.2 86.4 %all-gather.2.cloned.1.call-start = ((), (), s32[]{:S(2)}) async-start(), calls=%async_computation.1 | async-start | bytes 4325376 | tf_op jit(solution)/shard_map/all_gather | solution.py:47
  8.7 473.9 %reduce-scatter.2.cloned.1.call-start = ((), (), s32[]{:S(2)}) async-start(), calls=%async_computation.2 | async-start | bytes 270336 | tf_op jit(solution)/shard_map/reduce_scatter | solution.py:60
  98.8 176.3 %copy-start.3 = (f32[256,8]{0,1:T(8,128)S(1)}, f32[256,8]{0,1:T(8,128)}, u32[]{:S(2)}) copy-start(f32[256,8]{0,1:T(8,128)} %param.10) | copy-start | bytes 24580
  98.8 383.8 %copy-start.1 = (f32[256,8]{0,1:T(8,128)S(1)}, f32[256,8]{0,1:T(8,128)}, u32[]{:S(2)}) copy-start(f32[256,8]{0,1:T(8,128)} %param.11) | copy-start | bytes 24580
  98.8 464.4 %copy-start.4 = (f32[256,8]{0,1:T(8,128)S(1)}, f32[256,8]{0,1:T(8,128)}, u32[]{:S(2)}) copy-start(f32[256,8]{0,1:T(8,128)} %param.9) | copy-start | bytes 24580
  274.3 0.7 copy-start
  564.7 74.0 %copy-start.2 = (f32[256,8]{0,1:T(8,128)}, f32[256,8]{0,1:T(8,128)S(1)}, u32[]{:S(2)}) copy-start(f32[256,8]{0,1:T(8,128)S(1)} %get-tuple-element.169) | copy-start | bytes 24580
Sparse Core Ops, SparseCore 0:
  10.6 82.9 all-gather.1
  275.2 207.3 reduce-scatter.1
where the time goes:
time: 646 us
  waiting for transfers between devices  261 us (40%)
  blocking collectives  183 us (28%)
  matrix products  175 us (27%)
  between operations  14.1 us (2%)
  other arithmetic  9.27 us (1%)
    reduce_scatter x1, waiting for transfers between devices, local(): lax.psum_scatter(partial_sum, 'col', scatter_dimension=0, tiled=True)  207 us
    dot_general x8, matrix products, kernel_tile(): jnp.dot(row_s, col_s.T, precision=lax.Precision.HIGHEST, preferred_elemen...  107 us
    psum x1, blocking collectives, local(): norm_old = lax.psum(jnp.sum(residual * residual, axis=0), ('row', 'col'))  79.8 us
    psum x1, blocking collectives, local(): lax.psum(jnp.sum(new_residual * new_residual, axis=0), ('row', 'col'))  73.3 us
    dot_general x8, matrix products, kernel_product(): jnp.dot(kernel, col_v, precision=lax.Precision.HIGHEST, preferred_element...  68 us
    all_gather x1, waiting for transfers between devices, local(): row_points = lax.all_gather(points, 'col', axis=0, tiled=True)  53.8 us
    all_gather x1, blocking collectives, local(): lax.all_gather(direction, 'row', axis=0, tiled=True)  16 us
    all_gather x1, blocking collectives, local(): lax.all_gather(points, 'row', axis=0, tiled=True)  14 us
  transfers between devices with their start and end apart: 2, of which 2 were waited for; matrix products, arithmetic and copies ran while one was open for 0% of the time, Pallas kernels for 0%

commit v1 on v0

v1 whole, which is shorter than its diff:
```python
import functools
import math

import jax
import jax.numpy as jnp
from jax import lax
from jax.experimental import pallas as pl
from jax.experimental.pallas import tpu as pltpu
from jax.sharding import PartitionSpec as P

F = jnp.float32
H = jnp.bfloat16
MESH = pl.DeviceIdType.MESH
noise_level = 0.1
LOG2E = 1.0 / math.log(2.0)
SCALE = math.sqrt(5.0) * LOG2E
C1 = 3.0 * LOG2E
C0 = 3.0 * LOG2E * LOG2E
GAIN = 1.0 / C0
DIM = 32
RHS = 8
PACK = DIM + RHS
DEPTH = 256


def offsets(nz, ny):
    def hop(d, n):
        return min(d, n - d)

    whole, half, load = [], [], {}
    every = sorted(
        ((dz, dy) for dz in range(nz) for dy in range(ny)),
        key=lambda o: (hop(o[0], nz) + hop(o[1], ny), o),
    )

    def charge(o):
        dz, dy = o
        out = {}
        if dz and 2 * dz != nz:
            out["z+" if 2 * dz < nz else "z-"] = hop(dz, nz)
        if dy and 2 * dy != ny:
            out["y+" if 2 * dy < ny else "y-"] = hop(dy, ny)
        return out

    for o in every:
        back = ((-o[0]) % nz, (-o[1]) % ny)
        if o == (0, 0):
            continue
        if o == back:
            half.append(o)
            continue
        if o in whole or back in whole:
            continue

        def cost(cand):
            trial = dict(load)
            for key, hops in charge(cand).items():
                trial[key] = trial.get(key, 0) + hops
            return sum(v * v for v in trial.values())

        pick = min((o, back), key=cost)
        for key, hops in charge(pick).items():
            load[key] = load.get(key, 0) + hops
        whole.append(pick)
    return whole, half


def pieces(x):
    first = x.astype(H).astype(F)
    rest = x - first
    second = rest.astype(H).astype(F)
    third = (rest - second).astype(H).astype(F)
    return first, second, third


def norms(scaled):
    return jnp.sum(scaled * scaled, axis=0, keepdims=True)


def stack_left(block, width):
    scaled = block[:DIM, :]
    h, m, l = pieces(scaled)
    qh, qm, ql = pieces(norms(scaled))
    one = jnp.ones((1, width), F)
    zero = jnp.zeros((DEPTH - 6 * DIM - 8, width), F)
    tail = jnp.concatenate([qh, qm, ql, one, one, one, zero[:2]], axis=0)
    return jnp.concatenate([h, h, m, m, h, l, tail, zero], axis=0)


def stack_right(block, width):
    scaled = block[:DIM, :]
    h, m, l = pieces(scaled)
    h, m, l = -2.0 * h, -2.0 * m, -2.0 * l
    qh, qm, ql = pieces(norms(scaled))
    one = jnp.ones((1, width), F)
    zero = jnp.zeros((DEPTH - 6 * DIM - 8, width), F)
    tail = jnp.concatenate([one, one, one, qh, qm, ql, zero[:2]], axis=0)
    return jnp.concatenate([h, m, h, m, l, h, tail, zero], axis=0)


def two_pieces(v):
    first = v.astype(H).astype(F)
    return jnp.concatenate([first, v - first], axis=0)


def matern(x):
    x = jnp.maximum(x, 1e-30)
    t = x * lax.rsqrt(x)
    return (t * (t + C1) + C0) * jnp.exp2(-t)


def kernel(
    plan,
    pts_ref, inv_ref, sol_ref, res_ref, dir_ref,
    new_sol_ref, new_res_ref, new_dir_ref,
    pack, gather_a, gather_b, rows_b, vals_b, sums_b,
    send_a, send_b, back_a, back_b, red_row, red_z, red_y,
    ga_send, ga_recv, gb_send, gb_recv, ra_send, ra_recv, rb_send, rb_recv,
    rr_send, rr_recv, rz_send, rz_recv, ry_send, ry_recv,
):
    nr, nz, ny, whole, half = plan
    width = pts_ref.shape[1]
    r = lax.axis_index("row")
    c = lax.axis_index("col")
    z, y = c // ny, c % ny
    every = whole + half

    def shift(dz, dy):
        return (r, lax.rem(z + dz, nz) * ny + lax.rem(y + dy, ny))

    def row_shift(o):
        return (lax.rem(r + o, nr), c)

    def opposite(o):
        return ((nz - o[0]) % nz, (ny - o[1]) % ny)

    def remote(src, dst, send_sem, recv_sem, device):
        return pltpu.make_async_remote_copy(
            src_ref=src, dst_ref=dst, send_sem=send_sem, recv_sem=recv_sem,
            device_id=device, device_id_type=MESH,
        )

    barrier = pltpu.get_barrier_semaphore()
    for o in every:
        pl.semaphore_signal(barrier, inc=1, device_id=shift(*opposite(o)), device_id_type=MESH)
    for o in range(1, nr):
        pl.semaphore_signal(barrier, inc=1, device_id=row_shift(o), device_id_type=MESH)

    lengths = jnp.transpose(jnp.broadcast_to(inv_ref[...], (DIM, DIM)))[:, :1]
    pack[0:DIM, :] = pts_ref[...] * lengths * SCALE
    pack[DIM:PACK, :] = dir_ref[...]
    pl.semaphore_wait(barrier, len(every) + nr - 1)

    sends = []
    for o in range(1, nr):
        sends.append(remote(pack, gather_b.at[o], gb_send.at[o], gb_recv.at[o], row_shift(nr - o)))
    for i, o in enumerate(every):
        sends.append(remote(pack, gather_a.at[i], ga_send.at[i], ga_recv.at[i], shift(*o)))
    for copy in sends:
        copy.start()

    def prepare_b(o, block):
        at = pl.ds(pl.multiple_of(o * width, width), width)
        rows_b[at, :] = jnp.transpose(stack_right(block, width)).astype(H)
        vals_b[:, at] = two_pieces(block[DIM:PACK, :]).astype(H)

    prepare_b(0, pack[...])

    def arrive_b(o, carry):
        remote(pack, gather_b.at[o], gb_send.at[o], gb_recv.at[o], row_shift(1)).wait_recv()
        prepare_b(o, gather_b[o])
        return carry

    lax.fori_loop(1, nr, arrive_b, 0)
    sums_b[...] = jnp.zeros_like(sums_b)

    def prepare_a(block):
        left = stack_left(block, width).astype(H)
        vals = jnp.transpose(two_pieces(block[DIM:PACK, :])).astype(H)
        return left, jnp.concatenate([vals, vals], axis=0)

    def strip(left, rows):
        k = matern(jnp.dot(rows, left, preferred_element_type=F))
        high = k.astype(H)
        low = (k - high.astype(F)).astype(H)
        return high, low

    def down(values, high, low):
        out = jnp.dot(
            jnp.concatenate([values, values], axis=1),
            jnp.concatenate([high, low], axis=0),
            preferred_element_type=F,
        )
        return out[:RHS] + out[RHS:]

    def across(high, low, vals):
        return jnp.dot(jnp.concatenate([high, low], axis=1), vals, preferred_element_type=F)

    span = (nr // 2 + 1) * width
    left, vals = prepare_a(pack[...])
    high, low = strip(left, rows_b[:span, :])
    own = vals_b[:, :span]
    lane = lax.broadcasted_iota(jnp.int32, (1, span), 1)
    own = jnp.where(lane >= span - width, own.astype(F) * 0.5, own.astype(F)).astype(H)
    image = down(own, high, low)
    part = across(high[width:], low[width:], vals)
    line = lax.broadcasted_iota(jnp.int32, (span - width, 1), 0)
    part = jnp.where(line >= span - 2 * width, part * 0.5, part)
    sums_b[width:span, :] += part

    def table(i, entries):
        out = jnp.int32(entries[0])
        for n in range(1, len(entries)):
            out = jnp.where(i == n, jnp.int32(entries[n]), out)
        return out

    def give_back(i, value, entries, base):
        send_a[i] = value
        back = [opposite(o) for o in entries]
        dz = table(i - base, [o[0] for o in back])
        dy = table(i - base, [o[1] for o in back])
        remote(send_a.at[i], back_a.at[i], ra_send.at[i], ra_recv.at[i], shift(dz, dy)).start()

    def whole_strip(i, carry):
        remote(pack, gather_a.at[i], ga_send.at[i], ga_recv.at[i], row_shift(1)).wait_recv()
        left, vals = prepare_a(gather_a[i])
        high, low = strip(left, rows_b[...])
        give_back(i, down(vals_b[...], high, low), whole, 0)
        sums_b[...] += across(high, low, vals)
        return carry

    lax.fori_loop(0, len(whole), whole_strip, 0)

    halves = []
    for dz, dy in half:
        halves.append(2 * z // nz if dz else 2 * y // ny)

    def half_strip(i, carry):
        n = i - len(whole)
        remote(pack, gather_a.at[i], ga_send.at[i], ga_recv.at[i], row_shift(1)).wait_recv()
        left, vals = prepare_a(gather_a[i])
        side = halves[0]
        for k in range(1, len(halves)):
            side = jnp.where(n == k, halves[k], side)
        at = pl.ds(pl.multiple_of((1 - side) * width, width), nr // 2 * width)
        high, low = strip(left, rows_b[at, :])
        give_back(i, down(vals_b[:, at], high, low), half, len(whole))
        sums_b[at, :] += across(high, low, vals)
        return carry

    lax.fori_loop(len(whole), len(every), half_strip, 0)

    for o in range(nr):
        total = sums_b[o * width:(o + 1) * width, :]
        flipped = jnp.transpose(total)
        flipped = flipped[:RHS] + flipped[RHS:]
        if o == 0:
            image = image + flipped
        else:
            send_b[o] = flipped
            copy = remote(send_b.at[o], back_b.at[o], rb_send.at[o], rb_recv.at[o], row_shift(o))
            copy.start()
            sends.append(copy)

    for i in range(len(every)):
        copy = remote(send_a.at[i], back_a.at[i], ra_send.at[i], ra_recv.at[i], row_shift(1))
        copy.wait_recv()
        image = image + back_a[i]
    for o in range(1, nr):
        remote(send_b.at[o], back_b.at[o], rb_send.at[o], rb_recv.at[o], row_shift(1)).wait_recv()
        image = image + back_b[o]

    direction = dir_ref[...]
    residual = res_ref[...]
    image = GAIN * image + noise_level * direction

    def reduce_all(turn, value):
        for size, buf, ssem, rsem, mine, peer in (
            (nr, red_row, rr_send, rr_recv, r, lambda e: (lax.rem(r + e, nr), c)),
            (nz, red_z, rz_send, rz_recv, z, lambda e: shift(e, 0)),
            (ny, red_y, ry_send, ry_recv, y, lambda e: shift(0, e)),
        ):
            buf[turn, mine] = value
            for e in range(1, size):
                copy = remote(buf.at[turn, mine], buf.at[turn, mine], ssem.at[turn, e], rsem.at[turn, mine], peer(e))
                copy.start()
                sends.append(copy)
            for e in range(1, size):
                other = lax.rem(mine + e, size)
                remote(buf.at[turn, other], buf.at[turn, other], ssem.at[turn, e], rsem.at[turn, other], peer(e)).wait_recv()
            value = buf[turn, 0]
            for e in range(1, size):
                value = value + buf[turn, e]
        return value

    lane = lax.broadcasted_iota(jnp.int32, (RHS, 128), 1)
    old = jnp.sum(residual * residual, axis=1, keepdims=True)
    curve = jnp.sum(direction * image, axis=1, keepdims=True)
    both = reduce_all(0, jnp.where(lane == 0, old, curve))
    old, curve = both[:, 0:1], both[:, 1:2]
    step = old / curve
    new_sol_ref[...] = sol_ref[...] + step * direction
    fresh = residual - step * image
    new_res_ref[...] = fresh
    new = reduce_all(1, jnp.broadcast_to(jnp.sum(fresh * fresh, axis=1, keepdims=True), (RHS, 128)))[:, 0:1]
    new_dir_ref[...] = fresh + new / old * direction

    for copy in sends:
        copy.wait_send()

    def sent(i, carry):
        remote(send_a.at[i], back_a.at[i], ra_send.at[i], ra_recv.at[i], row_shift(1)).wait_send()
        return carry

    lax.fori_loop(0, len(every), sent, 0)


def solution(mesh):
    nr, nc = mesh.shape["row"], mesh.shape["col"]
    ny = 4 if nc == 32 else 2
    nz = nc // ny
    whole, half = offsets(nz, ny)
    na = len(whole) + len(half)

    def local(points, inv_length, solution_, residual, direction):
        width = points.shape[0]
        vmem = pl.BlockSpec(memory_space=pltpu.VMEM)
        dma = pltpu.SemaphoreType.DMA
        out = jax.ShapeDtypeStruct((RHS, width), F)
        flat = pl.pallas_call(
            functools.partial(kernel, (nr, nz, ny, whole, half)),
            out_shape=(out, out, out),
            in_specs=[vmem] * 5,
            out_specs=(vmem, vmem, vmem),
            scratch_shapes=[
                pltpu.VMEM((PACK, width), F),
                pltpu.VMEM((na, PACK, width), F),
                pltpu.VMEM((nr, PACK, width), F),
                pltpu.VMEM((nr * width, DEPTH), H),
                pltpu.VMEM((2 * RHS, nr * width), H),
                pltpu.VMEM((nr * width, 2 * RHS), F),
                pltpu.VMEM((na, RHS, width), F),
                pltpu.VMEM((nr, RHS, width), F),
                pltpu.VMEM((na, RHS, width), F),
                pltpu.VMEM((nr, RHS, width), F),
                pltpu.VMEM((2, nr, RHS, 128), F),
                pltpu.VMEM((2, nz, RHS, 128), F),
                pltpu.VMEM((2, ny, RHS, 128), F),
                dma((na,)), dma((na,)), dma((nr,)), dma((nr,)),
                dma((na,)), dma((na,)), dma((nr,)), dma((nr,)),
                dma((2, nr)), dma((2, nr)), dma((2, nz)), dma((2, nz)), dma((2, ny)), dma((2, ny)),
            ],
            compiler_params=pltpu.CompilerParams(
                collective_id=0, has_side_effects=True, vmem_limit_bytes=48 * 2**20
            ),
            cost_estimate=pl.CostEstimate(flops=2 * 10**10, bytes_accessed=10**6, transcendentals=2 * 10**7),
        )(points.T, inv_length.reshape(1, DIM), solution_.T, residual.T, direction.T)
        return tuple(x.T for x in flat)

    placed = (
        P(("row", "col"), None),
        P(),
        P(("row", "col"), None),
        P(("row", "col"), None),
        P(("row", "col"), None),
    )
    return jax.shard_map(
        local,
        mesh=mesh,
        in_specs=placed,
        out_specs=(P(("row", "col"), None),) * 3,
        check_vma=False,
    )
```

time: 646 us -> 81.8 us (0.13)
  waiting for transfers between devices: 261 us -> 0 us
  blocking collectives: 183 us -> 0 us
  matrix products: 175 us -> 0 us
  Pallas kernels: 0 us -> 76.3 us
  between operations: 14.1 us -> 0.66 us
  other arithmetic: 9.27 us -> 0 us
    reduce_scatter x1 -> x0, waiting for transfers between devices: 207 us -> none  [local(): lax.psum_scatter(partial_sum, 'col', scatter_dimension=0, tiled=True)]
    dot_general x16 -> x0, matrix products: 175 us -> none  [the longest x8 107 us: kernel_tile(): jnp.dot(row_s, col_s.T, precision=lax.Precision.HIGHEST, preferred_elemen...]
    psum x2 -> x0, blocking collectives: 153 us -> none  [the longest x1 79.8 us: local(): norm_old = lax.psum(jnp.sum(residual * residual, axis=0), ('row', 'col'))]
    pallas_call x0 -> x1, Pallas kernels: none -> 76.3 us  [local(): pl.pallas_call(functools.partial(kernel, (nr, nz, ny, whole, half)), out_...]
    all_gather x1 -> x0, waiting for transfers between devices: 53.8 us -> none  [local(): row_points = lax.all_gather(points, 'col', axis=0, tiled=True)]
    all_gather x2 -> x0, blocking collectives: 30 us -> none  [the longest x1 16 us: local(): lax.all_gather(direction, 'row', axis=0, tiled=True)]
    reduce_sum x5 -> x0, other arithmetic: 8.59 us -> none  [the longest x1 5.18 us: local(): row_q = jnp.sum(row_s * row_s, axis=1)]
  transfers between devices with their start and end apart: 2 -> 0, of which waited for: 2 -> 0; matrix products, arithmetic and copies ran while one was open for 0% -> 0% of each run, Pallas kernels for 0% -> 0%
where the time goes in v1:
time: 81.8 us; the launch traced here: 81.6 us
  Pallas kernels  76.3 us (93%)
  local copies, waits for them, and re-layouts  4.63 us (6%)
    pallas_call x1, Pallas kernels, local(): pl.pallas_call(functools.partial(kernel, (nr, nz, ny, whole, half)), out_...  76.3 us
    unnamed x13, local copies, waits for them, and re-layouts  4.63 us

profile of v1, /device:TPU:1, one launch (start us, length us, event | category | flops | bytes accessed | tf_op | source)
XLA Modules:
  0.0 81.6 jit_solution(1257576507995192482)
XLA Ops:
  0.6 0.0 copy-start.1
  0.6 0.0 copy-start.4
  0.7 0.7 copy-done.1
  1.3 0.0 copy-done.4
  1.3 0.0 copy-start
  1.3 0.8 copy-done
  2.1 0.0 copy-start.2
  2.1 0.7 copy-done.2
  2.8 0.0 copy-start.3
  2.8 0.7 copy-done.3
  3.5 76.3 %shard_map.76 = (f32[8,256]{1,0:T(8,128)S(1)}, f32[8,256]{1,0:T(8,128)S(1)}, f32[8,256]{1,0:T(8,128)S(1)}) custom-call(f32[32,256]{1,0:T(8,128)S(1)} %bitcast.11, f32[1,32]{1,0:T(1,128)S(1)} %bitcast.15, f32[8,256]{1,0:T(8,128)S(1)} %bitcast.12, f32[8,256]{1,0:T(8,128)S(1)} %bitcast.13, f32[8,256]{1,0:T(8,128)S(1)} %bitcast.14), custom_call_target="tpu_custom_call" | custom-call | flops 20000000000 | bytes 1000000 | tf_op jit(solution)/shard_map/pallas_call | solution.py:330
  79.8 0.6 copy.11
  80.4 0.6 copy.12
  81.0 0.6 copy.13
Async XLA Ops:
  0.6 0.7 copy-start.1
  0.6 0.7 copy-start.4
  1.3 0.8 copy-start
  2.1 0.7 copy-start.2
  2.8 0.7 copy-start.3

commit v2 on v1

--- a/solution.py
+++ b/solution.py
@@ -109,27 +109,79 @@
     return (t * (t + C1) + C0) * jnp.exp2(-t)
 
 
+def two_sum(a, b):
+    s = a + b
+    t = s - a
+    return s, (a - (s - t)) + (b - t)
+
+
+def split(a):
+    c = a * 4097.0
+    high = c - (c - a)
+    return high, a - high
+
+
+def two_product(a, b):
+    p = a * b
+    ah, al = split(a)
+    bh, bl = split(b)
+    return p, ((ah * bh - p) + ah * bl + al * bh) + al * bl
+
+
+def add_pairs(a, b):
+    s, e = two_sum(a[0], b[0])
+    return s, e + (a[1] + b[1])
+
+
+def settle(a):
+    return two_sum(a[0], a[1])
+
+
+def scale_pair(a, f):
+    p, e = two_product(a[0], f)
+    return settle((p, e + a[1] * f))
+
+
+def tree(items, join):
+    while len(items) > 1:
+        items = [join(*items[i:i + 2]) if i + 1 < len(items) else items[i] for i in range(0, len(items), 2)]
+    return items[0]
+
+
+def dot_pair(a, b):
+    p, e = two_product(a, b)
+    n = a.shape[1] // 128
+    pair = tree([(p[:, i * 128:(i + 1) * 128], e[:, i * 128:(i + 1) * 128]) for i in range(n)], add_pairs)
+    for shift in (64, 32, 16, 8, 4, 2, 1):
+        pair = add_pairs(pair, tuple(pltpu.roll(x, shift, 1) for x in pair))
+    return pair
+
+
 def kernel(
     plan,
+    pts_hbm, inv_hbm, sol_hbm, res_hbm, dir_hbm,
+    new_sol_ref, new_res_ref, new_dir_ref,
     pts_ref, inv_ref, sol_ref, res_ref, dir_ref,
-    new_sol_ref, new_res_ref, new_dir_ref,
     pack, gather_a, gather_b, rows_b, vals_b, sums_b,
-    send_a, send_b, back_a, back_b, red_row, red_z, red_y,
-    ga_send, ga_recv, gb_send, gb_recv, ra_send, ra_recv, rb_send, rb_recv,
-    rr_send, rr_recv, rz_send, rz_recv, ry_send, ry_recv,
+    send_a, send_b, back_a, back_b, red_row, red_col,
+    in_sem, ga_send, ga_recv, gb_send, gb_recv, ra_send, ra_recv, rb_send, rb_recv,
+    rr_send, rr_recv, rc_send, rc_recv,
 ):
     nr, nz, ny, whole, half = plan
+    nx = nr // 2
     width = pts_ref.shape[1]
     r = lax.axis_index("row")
     c = lax.axis_index("col")
     z, y = c // ny, c % ny
+    x, core = r // 2, r % 2
     every = whole + half
 
     def shift(dz, dy):
         return (r, lax.rem(z + dz, nz) * ny + lax.rem(y + dy, ny))
 
-    def row_shift(o):
-        return (lax.rem(r + o, nr), c)
+    def row_shift(o, sign=1):
+        dx = (o // 2) if sign > 0 else (nx - o // 2) % nx
+        return (lax.rem(x + dx, nx) * 2 + lax.rem(core + o % 2, 2), c)
 
     def opposite(o):
         return ((nz - o[0]) % nz, (ny - o[1]) % ny)
@@ -146,6 +198,18 @@
     for o in range(1, nr):
         pl.semaphore_signal(barrier, inc=1, device_id=row_shift(o), device_id_type=MESH)
 
+    loads = [
+        pltpu.make_async_copy(src, dst, in_sem.at[i])
+        for i, (src, dst) in enumerate((
+            (pts_hbm, pts_ref), (dir_hbm, dir_ref), (inv_hbm, inv_ref), (res_hbm, res_ref), (sol_hbm, sol_ref),
+        ))
+    ]
+    for copy in loads:
+        copy.start()
+    sums_b[...] = jnp.zeros_like(sums_b)
+    for copy in loads:
+        copy.wait()
+
     lengths = jnp.transpose(jnp.broadcast_to(inv_ref[...], (DIM, DIM)))[:, :1]
     pack[0:DIM, :] = pts_ref[...] * lengths * SCALE
     pack[DIM:PACK, :] = dir_ref[...]
@@ -153,7 +217,7 @@
 
     sends = []
     for o in range(1, nr):
-        sends.append(remote(pack, gather_b.at[o], gb_send.at[o], gb_recv.at[o], row_shift(nr - o)))
+        sends.append(remote(pack, gather_b.at[o], gb_send.at[o], gb_recv.at[o], row_shift(o, -1)))
     for i, o in enumerate(every):
         sends.append(remote(pack, gather_a.at[i], ga_send.at[i], ga_recv.at[i], shift(*o)))
     for copy in sends:
@@ -172,7 +236,6 @@
         return carry
 
     lax.fori_loop(1, nr, arrive_b, 0)
-    sums_b[...] = jnp.zeros_like(sums_b)
 
     def prepare_a(block):
         left = stack_left(block, width).astype(H)
@@ -196,18 +259,6 @@
     def across(high, low, vals):
         return jnp.dot(jnp.concatenate([high, low], axis=1), vals, preferred_element_type=F)
 
-    span = (nr // 2 + 1) * width
-    left, vals = prepare_a(pack[...])
-    high, low = strip(left, rows_b[:span, :])
-    own = vals_b[:, :span]
-    lane = lax.broadcasted_iota(jnp.int32, (1, span), 1)
-    own = jnp.where(lane >= span - width, own.astype(F) * 0.5, own.astype(F)).astype(H)
-    image = down(own, high, low)
-    part = across(high[width:], low[width:], vals)
-    line = lax.broadcasted_iota(jnp.int32, (span - width, 1), 0)
-    part = jnp.where(line >= span - 2 * width, part * 0.5, part)
-    sums_b[width:span, :] += part
-
     def table(i, entries):
         out = jnp.int32(entries[0])
         for n in range(1, len(entries)):
@@ -242,7 +293,7 @@
         side = halves[0]
         for k in range(1, len(halves)):
             side = jnp.where(n == k, halves[k], side)
-        at = pl.ds(pl.multiple_of((1 - side) * width, width), nr // 2 * width)
+        at = pl.ds(pl.multiple_of((1 - side) * 2 * width, 2 * width), nr // 2 * width)
         high, low = strip(left, rows_b[at, :])
         give_back(i, down(vals_b[:, at], high, low), half, len(whole))
         sums_b[at, :] += across(high, low, vals)
@@ -250,17 +301,18 @@
 
     lax.fori_loop(len(whole), len(every), half_strip, 0)
 
-    for o in range(nr):
-        total = sums_b[o * width:(o + 1) * width, :]
-        flipped = jnp.transpose(total)
-        flipped = flipped[:RHS] + flipped[RHS:]
-        if o == 0:
-            image = image + flipped
-        else:
-            send_b[o] = flipped
-            copy = remote(send_b.at[o], back_b.at[o], rb_send.at[o], rb_recv.at[o], row_shift(o))
-            copy.start()
-            sends.append(copy)
+    for o in range(1, nr):
+        flipped = jnp.transpose(sums_b[o * width:(o + 1) * width, :])
+        send_b[o] = flipped[:RHS] + flipped[RHS:]
+        copy = remote(send_b.at[o], back_b.at[o], rb_send.at[o], rb_recv.at[o], row_shift(o))
+        copy.start()
+        sends.append(copy)
+    flipped = jnp.transpose(sums_b[0:width, :])
+    image = flipped[:RHS] + flipped[RHS:]
+
+    left, _ = prepare_a(pack[...])
+    high, low = strip(left, rows_b[...])
+    image = image + down(vals_b[...], high, low)
 
     for i in range(len(every)):
         copy = remote(send_a.at[i], back_a.at[i], ra_send.at[i], ra_recv.at[i], row_shift(1))
@@ -274,36 +326,40 @@
     residual = res_ref[...]
     image = GAIN * image + noise_level * direction
 
-    def reduce_all(turn, value):
-        for size, buf, ssem, rsem, mine, peer in (
-            (nr, red_row, rr_send, rr_recv, r, lambda e: (lax.rem(r + e, nr), c)),
-            (nz, red_z, rz_send, rz_recv, z, lambda e: shift(e, 0)),
-            (ny, red_y, ry_send, ry_recv, y, lambda e: shift(0, e)),
-        ):
-            buf[turn, mine] = value
-            for e in range(1, size):
-                copy = remote(buf.at[turn, mine], buf.at[turn, mine], ssem.at[turn, e], rsem.at[turn, mine], peer(e))
-                copy.start()
-                sends.append(copy)
-            for e in range(1, size):
-                other = lax.rem(mine + e, size)
-                remote(buf.at[turn, other], buf.at[turn, other], ssem.at[turn, e], rsem.at[turn, other], peer(e)).wait_recv()
-            value = buf[turn, 0]
-            for e in range(1, size):
-                value = value + buf[turn, e]
-        return value
-
     lane = lax.broadcasted_iota(jnp.int32, (RHS, 128), 1)
-    old = jnp.sum(residual * residual, axis=1, keepdims=True)
-    curve = jnp.sum(direction * image, axis=1, keepdims=True)
-    both = reduce_all(0, jnp.where(lane == 0, old, curve))
-    old, curve = both[:, 0:1], both[:, 1:2]
-    step = old / curve
+    pairs = [dot_pair(residual, residual), dot_pair(direction, image), dot_pair(residual, image), dot_pair(image, image)]
+    mixed = jnp.zeros((RHS, 128), F)
+    for q, pair in enumerate(pairs):
+        mixed = jnp.where(lane == q, pair[0], jnp.where(lane == q + 4, pair[1], mixed))
+    value = jnp.sum(pltpu.roll(mixed, 0, 1, stride=8, stride_axis=0), axis=0, keepdims=True)
+    first = lax.broadcasted_iota(jnp.int32, (1, 128), 1) % 8 < 4
+
+    for size, buf, ssem, rsem, mine, peer in (
+        (nr, red_row, rr_send, rr_recv, r, lambda e: (lax.rem(r + e, nr), c)),
+        (nz * ny, red_col, rc_send, rc_recv, c, lambda e: (r, lax.rem(c + e, nz * ny))),
+    ):
+        buf[mine] = value
+        for e in range(1, size):
+            copy = remote(buf.at[mine], buf.at[mine], ssem.at[e], rsem.at[mine], peer(e))
+            copy.start()
+            sends.append(copy)
+        for e in range(1, size):
+            other = lax.rem(mine + e, size)
+            remote(buf.at[other], buf.at[other], ssem.at[e], rsem.at[other], peer(e)).wait_recv()
+        total, error = tree([(buf[e], jnp.zeros((1, 128), F)) for e in range(size)], add_pairs)
+        value = jnp.where(first, total, total + pltpu.roll(error, 4, 1))
+
+    place = lane - 8 * lax.broadcasted_iota(jnp.int32, (RHS, 128), 0)
+    sums = [jnp.sum(jnp.where(place == q, value, 0.0), axis=1, keepdims=True) for q in range(8)]
+    old, curve, cross, square = (settle((sums[q], sums[q + 4])) for q in range(4))
+    step = old[0] / curve[0]
+    change = scale_pair(square, -step)
+    change = scale_pair(add_pairs((2.0 * cross[0], 2.0 * cross[1]), change), -step)
+    new = settle(add_pairs(old, change))[0]
+    fresh = residual - step * image
     new_sol_ref[...] = sol_ref[...] + step * direction
-    fresh = residual - step * image
     new_res_ref[...] = fresh
-    new = reduce_all(1, jnp.broadcast_to(jnp.sum(fresh * fresh, axis=1, keepdims=True), (RHS, 128)))[:, 0:1]
-    new_dir_ref[...] = fresh + new / old * direction
+    new_dir_ref[...] = fresh + new / old[0] * direction
 
     for copy in sends:
         copy.wait_send()
@@ -330,9 +386,14 @@
         flat = pl.pallas_call(
             functools.partial(kernel, (nr, nz, ny, whole, half)),
             out_shape=(out, out, out),
-            in_specs=[vmem] * 5,
+            in_specs=[pl.BlockSpec(memory_space=pltpu.HBM)] * 5,
             out_specs=(vmem, vmem, vmem),
             scratch_shapes=[
+                pltpu.VMEM((DIM, width), F),
+                pltpu.VMEM((1, DIM), F),
+                pltpu.VMEM((RHS, width), F),
+                pltpu.VMEM((RHS, width), F),
+                pltpu.VMEM((RHS, width), F),
                 pltpu.VMEM((PACK, width), F),
                 pltpu.VMEM((na, PACK, width), F),
                 pltpu.VMEM((nr, PACK, width), F),
@@ -343,12 +404,12 @@
                 pltpu.VMEM((nr, RHS, width), F),
                 pltpu.VMEM((na, RHS, width), F),
                 pltpu.VMEM((nr, RHS, width), F),
-                pltpu.VMEM((2, nr, RHS, 128), F),
-                pltpu.VMEM((2, nz, RHS, 128), F),
-                pltpu.VMEM((2, ny, RHS, 128), F),
+                pltpu.VMEM((nr, 1, 128), F),
+                pltpu.VMEM((nc, 1, 128), F),
+                dma((5,)),
                 dma((na,)), dma((na,)), dma((nr,)), dma((nr,)),
                 dma((na,)), dma((na,)), dma((nr,)), dma((nr,)),
-                dma((2, nr)), dma((2, nr)), dma((2, nz)), dma((2, nz)), dma((2, ny)), dma((2, ny)),
+                dma((nr,)), dma((nr,)), dma((nc,)), dma((nc,)),
             ],
             compiler_params=pltpu.CompilerParams(
                 collective_id=0, has_side_effects=True, vmem_limit_bytes=48 * 2**20

time: 81.8 us -> 68.8 us (0.84)
  Pallas kernels: 76.3 us -> 63.2 us
    pallas_call x1, Pallas kernels: 76.3 us -> 63.2 us  [local(): pl.pallas_call(functools.partial(kernel, (nr, nz, ny, whole, half)), out_...]
where the time goes in v2:
time: 68.8 us; the launch traced here: 68.5 us
  Pallas kernels  63.2 us (92%)
  local copies, waits for them, and re-layouts  4.63 us (7%)
    pallas_call x1, Pallas kernels, local(): pl.pallas_call(functools.partial(kernel, (nr, nz, ny, whole, half)), out_...  63.2 us
    unnamed x13, local copies, waits for them, and re-layouts  4.63 us

profile of v2, /device:TPU:1, one launch (start us, length us, event | category | flops | bytes accessed | tf_op | source)
XLA Modules:
  0.0 68.5 jit_solution(14472415707255442037)
XLA Ops:
  0.6 0.0 copy-start.1
  0.6 0.0 copy-start.4
  0.7 0.7 copy-done.1
  1.3 0.0 copy-done.4
  1.3 0.0 copy-start
  1.3 0.8 %copy-done = f32[256,32]{0,1:T(8,128)S(1)} copy-done((f32[256,32]{0,1:T(8,128)S(1)}, f32[256,32]{0,1:T(8,128)}, u32[]{:S(2)}) %copy-start) | copy-done | bytes 32792
  2.1 0.0 copy-start.2
  2.1 0.7 %copy-done.2 = f32[256,8]{0,1:T(8,128)S(1)} copy-done((f32[256,8]{0,1:T(8,128)S(1)}, f32[256,8]{0,1:T(8,128)}, u32[]{:S(2)}) %copy-start.2) | copy-done | bytes 8216
  2.8 0.0 copy-start.3
  2.8 0.7 %copy-done.3 = f32[256,8]{0,1:T(8,128)S(1)} copy-done((f32[256,8]{0,1:T(8,128)S(1)}, f32[256,8]{0,1:T(8,128)}, u32[]{:S(2)}) %copy-start.3) | copy-done | bytes 8216
  3.5 63.2 %shard_map.76 = (f32[8,256]{1,0:T(8,128)S(1)}, f32[8,256]{1,0:T(8,128)S(1)}, f32[8,256]{1,0:T(8,128)S(1)}) custom-call(f32[32,256]{1,0:T(8,128)S(1)} %bitcast.11, f32[1,32]{1,0:T(1,128)S(1)} %bitcast.15, f32[8,256]{1,0:T(8,128)S(1)} %bitcast.12, f32[8,256]{1,0:T(8,128)S(1)} %bitcast.13, f32[8,256]{1,0:T(8,128)S(1)} %bitcast.14), custom_call_target="tpu_custom_call" | custom-call | flops 20000000000 | bytes 1000000 | tf_op jit(solution)/shard_map/pallas_call | solution.py:386
  66.7 0.6 copy.11
  67.3 0.6 copy.12
  67.9 0.6 copy.13
Async XLA Ops:
  0.6 0.7 %copy-start.1 = (f32[256,8]{0,1:T(8,128)S(1)}, f32[256,8]{0,1:T(8,128)}, u32[]{:S(2)}) copy-start(f32[256,8]{0,1:T(8,128)} %param.7) | copy-start | bytes 24580
  0.6 0.7 %copy-start.4 = (f32[32]{0:T(128)S(1)}, f32[32]{0:T(128)}, u32[]{:S(2)}) copy-start(f32[32]{0:T(128)} %param.6) | copy-start | bytes 388
  1.3 0.8 %copy-start = (f32[256,32]{0,1:T(8,128)S(1)}, f32[256,32]{0,1:T(8,128)}, u32[]{:S(2)}) copy-start(f32[256,32]{0,1:T(8,128)} %param.5) | copy-start | bytes 98308
  2.1 0.7 %copy-start.2 = (f32[256,8]{0,1:T(8,128)S(1)}, f32[256,8]{0,1:T(8,128)}, u32[]{:S(2)}) copy-start(f32[256,8]{0,1:T(8,128)} %param.8) | copy-start | bytes 24580
  2.8 0.7 %copy-start.3 = (f32[256,8]{0,1:T(8,128)S(1)}, f32[256,8]{0,1:T(8,128)}, u32[]{:S(2)}) copy-start(f32[256,8]{0,1:T(8,128)} %param.9) | copy-start | bytes 24580

commit v3 on v2

--- a/solution.py
+++ b/solution.py
@@ -160,7 +160,7 @@
 def kernel(
     plan,
     pts_hbm, inv_hbm, sol_hbm, res_hbm, dir_hbm,
-    new_sol_ref, new_res_ref, new_dir_ref,
+    out_ref,
     pts_ref, inv_ref, sol_ref, res_ref, dir_ref,
     pack, gather_a, gather_b, rows_b, vals_b, sums_b,
     send_a, send_b, back_a, back_b, red_row, red_col,
@@ -357,9 +357,9 @@
     change = scale_pair(add_pairs((2.0 * cross[0], 2.0 * cross[1]), change), -step)
     new = settle(add_pairs(old, change))[0]
     fresh = residual - step * image
-    new_sol_ref[...] = sol_ref[...] + step * direction
-    new_res_ref[...] = fresh
-    new_dir_ref[...] = fresh + new / old[0] * direction
+    out_ref[0:8] = sol_ref[...] + step * direction
+    out_ref[8:16] = fresh
+    out_ref[16:24] = fresh + new / old[0] * direction
 
     for copy in sends:
         copy.wait_send()
@@ -382,12 +382,12 @@
         width = points.shape[0]
         vmem = pl.BlockSpec(memory_space=pltpu.VMEM)
         dma = pltpu.SemaphoreType.DMA
-        out = jax.ShapeDtypeStruct((RHS, width), F)
+        out = jax.ShapeDtypeStruct((3 * RHS, width), F)
         flat = pl.pallas_call(
             functools.partial(kernel, (nr, nz, ny, whole, half)),
-            out_shape=(out, out, out),
+            out_shape=out,
             in_specs=[pl.BlockSpec(memory_space=pltpu.HBM)] * 5,
-            out_specs=(vmem, vmem, vmem),
+            out_specs=vmem,
             scratch_shapes=[
                 pltpu.VMEM((DIM, width), F),
                 pltpu.VMEM((1, DIM), F),
@@ -412,11 +412,11 @@
                 dma((nr,)), dma((nr,)), dma((nc,)), dma((nc,)),
             ],
             compiler_params=pltpu.CompilerParams(
-                collective_id=0, has_side_effects=True, vmem_limit_bytes=48 * 2**20
+                collective_id=0, has_side_effects=True
             ),
             cost_estimate=pl.CostEstimate(flops=2 * 10**10, bytes_accessed=10**6, transcendentals=2 * 10**7),
         )(points.T, inv_length.reshape(1, DIM), solution_.T, residual.T, direction.T)
-        return tuple(x.T for x in flat)
+        return flat[0:8].T, flat[8:16].T, flat[16:24].T
 
     placed = (
         P(("row", "col"), None),

time: 68.8 us -> 66.2 us (0.962)
  local copies, waits for them, and re-layouts: 4.63 us -> 1.34 us
  Pallas kernels: 63.2 us -> 64.1 us
    unnamed x13 -> x0, local copies, waits for them, and re-layouts: 4.63 us -> none
    transpose x0 -> x1, local copies, waits for them, and re-layouts: none -> 1.34 us  [local(): return (flat[0:8].T, flat[8:16].T, flat[16:24].T)]
    pallas_call x1, Pallas kernels: 63.2 us -> 64.1 us  [local(): pl.pallas_call(functools.partial(kernel, (nr, nz, ny, whole, half)), out_...]
where the time goes in v3:
time: 66.2 us; the launch traced here: 66.1 us
  Pallas kernels  64.1 us (97%)
  local copies, waits for them, and re-layouts  1.34 us (2%)
    pallas_call x1, Pallas kernels, local(): pl.pallas_call(functools.partial(kernel, (nr, nz, ny, whole, half)), out_...  64.1 us
    transpose x1, local copies, waits for them, and re-layouts, local(): return (flat[0:8].T, flat[8:16].T, flat[16:24].T)  1.34 us

profile of v3, /device:TPU:1, one launch (start us, length us, event | category | flops | bytes accessed | tf_op | source)
XLA Modules:
  0.0 66.1 jit_solution(700493811962989906)
XLA Ops:
  0.6 64.1 %shard_map.76 = f32[24,256]{1,0:T(8,128)} custom-call(f32[32,256]{1,0:T(8,128)} %bitcast.11, f32[1,32]{1,0:T(1,128)} %bitcast.15, f32[8,256]{1,0:T(8,128)} %bitcast.12, f32[8,256]{1,0:T(8,128)} %bitcast.13, f32[8,256]{1,0:T(8,128)} %bitcast.14), custom_call_target="tpu_custom_call" | custom-call | flops 20000000000 | bytes 1000000 | tf_op jit(solution)/shard_map/pallas_call | solution.py:386
  64.7 1.3 %slice_bitcast_fusion = (f32[256,8]{0,1:T(8,128)}, f32[256,8]{0,1:T(8,128)}, f32[256,8]{0,1:T(8,128)}) fusion(f32[24,256]{1,0:T(8,128)} %shard_map.76), kind=kLoop, calls=%fused_computation | loop fusion | bytes 49152 | tf_op jit(solution)/shard_map/transpose | solution.py:419

commit v4 on v3

--- a/solution.py
+++ b/solution.py
@@ -20,6 +20,7 @@
 DIM = 32
 RHS = 8
 PACK = DIM + RHS
+NEAR = 2
 DEPTH = 256
 
 
@@ -215,11 +216,13 @@
     pack[DIM:PACK, :] = dir_ref[...]
     pl.semaphore_wait(barrier, len(every) + nr - 1)
 
-    sends = []
-    for o in range(1, nr):
-        sends.append(remote(pack, gather_b.at[o], gb_send.at[o], gb_recv.at[o], row_shift(o, -1)))
-    for i, o in enumerate(every):
-        sends.append(remote(pack, gather_a.at[i], ga_send.at[i], ga_recv.at[i], shift(*o)))
+    to_row = [
+        remote(pack, gather_b.at[o], gb_send.at[o], gb_recv.at[o], row_shift(o, -1)) for o in range(1, nr)
+    ]
+    to_col = [
+        remote(pack, gather_a.at[i], ga_send.at[i], ga_recv.at[i], shift(*o)) for i, o in enumerate(every)
+    ]
+    sends = to_row[:1] + to_col[:2] + to_row[1:] + to_col[2:]
     for copy in sends:
         copy.start()
 
@@ -235,7 +238,7 @@
         prepare_b(o, gather_b[o])
         return carry
 
-    lax.fori_loop(1, nr, arrive_b, 0)
+    arrive_b(1, 0)
 
     def prepare_a(block):
         left = stack_left(block, width).astype(H)
@@ -272,15 +275,35 @@
         dy = table(i - base, [o[1] for o in back])
         remote(send_a.at[i], back_a.at[i], ra_send.at[i], ra_recv.at[i], shift(dz, dy)).start()
 
+    def work(i, at):
+        left, vals = prepare_a(gather_a[i])
+        high, low = strip(left, rows_b[at, :])
+        sums_b[at, :] += across(high, low, vals)
+        return down(vals_b[:, at], high, low)
+
+    def arrive_a(i):
+        remote(pack, gather_a.at[i], ga_send.at[i], ga_recv.at[i], row_shift(1)).wait_recv()
+
+    near = min(NEAR, len(whole))
+    chip, rest = slice(0, 2 * width), slice(2 * width, nr * width)
+
+    def near_strip(i, carry):
+        arrive_a(i)
+        send_a[i] = work(i, chip)
+        return carry
+
     def whole_strip(i, carry):
-        remote(pack, gather_a.at[i], ga_send.at[i], ga_recv.at[i], row_shift(1)).wait_recv()
-        left, vals = prepare_a(gather_a[i])
-        high, low = strip(left, rows_b[...])
-        give_back(i, down(vals_b[...], high, low), whole, 0)
-        sums_b[...] += across(high, low, vals)
-        return carry
-
-    lax.fori_loop(0, len(whole), whole_strip, 0)
+        arrive_a(i)
+        give_back(i, work(i, slice(None)), whole, 0)
+        return carry
+
+    def last_strip(i, carry):
+        give_back(i, send_a[i] + work(i, rest), whole, 0)
+        return carry
+
+    lax.fori_loop(0, near, near_strip, 0)
+    lax.fori_loop(2, nr, arrive_b, 0)
+    lax.fori_loop(near, len(whole), whole_strip, 0)
 
     halves = []
     for dz, dy in half:
@@ -288,18 +311,16 @@
 
     def half_strip(i, carry):
         n = i - len(whole)
-        remote(pack, gather_a.at[i], ga_send.at[i], ga_recv.at[i], row_shift(1)).wait_recv()
-        left, vals = prepare_a(gather_a[i])
+        arrive_a(i)
         side = halves[0]
         for k in range(1, len(halves)):
             side = jnp.where(n == k, halves[k], side)
         at = pl.ds(pl.multiple_of((1 - side) * 2 * width, 2 * width), nr // 2 * width)
-        high, low = strip(left, rows_b[at, :])
-        give_back(i, down(vals_b[:, at], high, low), half, len(whole))
-        sums_b[at, :] += across(high, low, vals)
+        give_back(i, work(i, at), half, len(whole))
         return carry
 
     lax.fori_loop(len(whole), len(every), half_strip, 0)
+    lax.fori_loop(0, near, last_strip, 0)
 
     for o in range(1, nr):
         flipped = jnp.transpose(sums_b[o * width:(o + 1) * width, :])

time: 66.2 us -> 60.7 us (0.917)
  Pallas kernels: 64.1 us -> 58.6 us
    pallas_call x1, Pallas kernels: 64.1 us -> 58.6 us  [local(): pl.pallas_call(functools.partial(kernel, (nr, nz, ny, whole, half)), out_...]
where the time goes in v4:
time: 60.7 us; the launch traced here: 60.5 us
  Pallas kernels  58.6 us (97%)
  local copies, waits for them, and re-layouts  1.34 us (2%)
  between operations  0.64 us (1%)
    pallas_call x1, Pallas kernels, local(): pl.pallas_call(functools.partial(kernel, (nr, nz, ny, whole, half)), out_...  58.6 us
    transpose x1, local copies, waits for them, and re-layouts, local(): return (flat[0:8].T, flat[8:16].T, flat[16:24].T)  1.34 us

profile of v4, /device:TPU:1, one launch (start us, length us, event | category | flops | bytes accessed | tf_op | source)
XLA Modules:
  0.0 60.5 jit_solution(4052774795394036896)
XLA Ops:
  0.6 58.6 %shard_map.76 = f32[24,256]{1,0:T(8,128)} custom-call(f32[32,256]{1,0:T(8,128)} %bitcast.11, f32[1,32]{1,0:T(1,128)} %bitcast.15, f32[8,256]{1,0:T(8,128)} %bitcast.12, f32[8,256]{1,0:T(8,128)} %bitcast.13, f32[8,256]{1,0:T(8,128)} %bitcast.14), custom_call_target="tpu_custom_call" | custom-call | flops 20000000000 | bytes 1000000 | tf_op jit(solution)/shard_map/pallas_call | solution.py:407
  59.2 1.3 %slice_bitcast_fusion = (f32[256,8]{0,1:T(8,128)}, f32[256,8]{0,1:T(8,128)}, f32[256,8]{0,1:T(8,128)}) fusion(f32[24,256]{1,0:T(8,128)} %shard_map.76), kind=kLoop, calls=%fused_computation | loop fusion | bytes 49152 | tf_op jit(solution)/shard_map/transpose | solution.py:440

commit v5 on v4

--- a/solution.py
+++ b/solution.py
@@ -10,13 +10,15 @@
 
 F = jnp.float32
 H = jnp.bfloat16
+Q = jnp.float8_e4m3fn
 MESH = pl.DeviceIdType.MESH
 noise_level = 0.1
 LOG2E = 1.0 / math.log(2.0)
 SCALE = math.sqrt(5.0) * LOG2E
 C1 = 3.0 * LOG2E
 C0 = 3.0 * LOG2E * LOG2E
-GAIN = 1.0 / C0
+LIFT = 14.0
+GAIN = 2.0 ** -LIFT / C0
 DIM = 32
 RHS = 8
 PACK = DIM + RHS
@@ -104,10 +106,15 @@
     return jnp.concatenate([first, v - first], axis=0)
 
 
+def two_eighths(v):
+    first = v.astype(Q).astype(F)
+    return jnp.concatenate([first, v - first, jnp.zeros_like(v), jnp.zeros_like(v)], axis=0)
+
+
 def matern(x):
     x = jnp.maximum(x, 1e-30)
     t = x * lax.rsqrt(x)
-    return (t * (t + C1) + C0) * jnp.exp2(-t)
+    return (t * (t + C1) + C0) * jnp.exp2(LIFT - t)
 
 
 def two_sum(a, b):
@@ -163,7 +170,7 @@
     pts_hbm, inv_hbm, sol_hbm, res_hbm, dir_hbm,
     out_ref,
     pts_ref, inv_ref, sol_ref, res_ref, dir_ref,
-    pack, gather_a, gather_b, rows_b, vals_b, sums_b,
+    pack, gather_a, gather_b, rows_b, vals_b, eighth_b, sums_b,
     send_a, send_b, back_a, back_b, red_row, red_col,
     in_sem, ga_send, ga_recv, gb_send, gb_recv, ra_send, ra_recv, rb_send, rb_recv,
     rr_send, rr_recv, rc_send, rc_recv,
@@ -230,6 +237,7 @@
         at = pl.ds(pl.multiple_of(o * width, width), width)
         rows_b[at, :] = jnp.transpose(stack_right(block, width)).astype(H)
         vals_b[:, at] = two_pieces(block[DIM:PACK, :]).astype(H)
+        eighth_b[:, at] = two_eighths(block[DIM:PACK, :]).astype(Q)
 
     prepare_b(0, pack[...])
 
@@ -243,24 +251,17 @@
     def prepare_a(block):
         left = stack_left(block, width).astype(H)
         vals = jnp.transpose(two_pieces(block[DIM:PACK, :])).astype(H)
-        return left, jnp.concatenate([vals, vals], axis=0)
+        eighth = jnp.transpose(two_eighths(block[DIM:PACK, :])[:2 * RHS]).astype(Q)
+        return left, vals, eighth
 
     def strip(left, rows):
         k = matern(jnp.dot(rows, left, preferred_element_type=F))
         high = k.astype(H)
-        low = (k - high.astype(F)).astype(H)
+        low = (k - high.astype(F)).astype(Q)
         return high, low
 
-    def down(values, high, low):
-        out = jnp.dot(
-            jnp.concatenate([values, values], axis=1),
-            jnp.concatenate([high, low], axis=0),
-            preferred_element_type=F,
-        )
-        return out[:RHS] + out[RHS:]
-
-    def across(high, low, vals):
-        return jnp.dot(jnp.concatenate([high, low], axis=1), vals, preferred_element_type=F)
+    def product(a, b):
+        return jnp.dot(a, b, preferred_element_type=F)
 
     def table(i, entries):
         out = jnp.int32(entries[0])
@@ -276,10 +277,13 @@
         remote(send_a.at[i], back_a.at[i], ra_send.at[i], ra_recv.at[i], shift(dz, dy)).start()
 
     def work(i, at):
-        left, vals = prepare_a(gather_a[i])
+        left, vals, eighth = prepare_a(gather_a[i])
         high, low = strip(left, rows_b[at, :])
-        sums_b[at, :] += across(high, low, vals)
-        return down(vals_b[:, at], high, low)
+        sums_b[at, :] += product(high, vals)
+        out = product(vals_b[:, at], high)
+        sums_b[at, :] += product(low, eighth)
+        fine = product(eighth_b[:, at], low)
+        return out[:RHS] + out[RHS:] + (fine[:RHS] + fine[RHS:2 * RHS])
 
     def arrive_a(i):
         remote(pack, gather_a.at[i], ga_send.at[i], ga_recv.at[i], row_shift(1)).wait_recv()
@@ -331,9 +335,11 @@
     flipped = jnp.transpose(sums_b[0:width, :])
     image = flipped[:RHS] + flipped[RHS:]
 
-    left, _ = prepare_a(pack[...])
+    left, _, _ = prepare_a(pack[...])
     high, low = strip(left, rows_b[...])
-    image = image + down(vals_b[...], high, low)
+    out = product(vals_b[...], high)
+    fine = product(eighth_b[...], low)
+    image = image + (out[:RHS] + out[RHS:] + (fine[:RHS] + fine[RHS:2 * RHS]))
 
     for i in range(len(every)):
         copy = remote(send_a.at[i], back_a.at[i], ra_send.at[i], ra_recv.at[i], row_shift(1))
@@ -420,6 +426,7 @@
                 pltpu.VMEM((nr, PACK, width), F),
                 pltpu.VMEM((nr * width, DEPTH), H),
                 pltpu.VMEM((2 * RHS, nr * width), H),
+                pltpu.VMEM((4 * RHS, nr * width), Q),
                 pltpu.VMEM((nr * width, 2 * RHS), F),
                 pltpu.VMEM((na, RHS, width), F),
                 pltpu.VMEM((nr, RHS, width), F),

time: 60.7 us -> 57.4 us (0.946)
  Pallas kernels: 58.6 us -> 55.2 us
    pallas_call x1, Pallas kernels: 58.6 us -> 55.2 us  [local(): pl.pallas_call(functools.partial(kernel, (nr, nz, ny, whole, half)), out_...]
where the time goes in v5:
time: 57.4 us; the launch traced here: 57.2 us
  Pallas kernels  55.2 us (96%)
  local copies, waits for them, and re-layouts  1.34 us (2%)
  between operations  0.64 us (1%)
    pallas_call x1, Pallas kernels, local(): pl.pallas_call(functools.partial(kernel, (nr, nz, ny, whole, half)), out_...  55.2 us
    transpose x1, local copies, waits for them, and re-layouts, local(): return (flat[0:8].T, flat[8:16].T, flat[16:24].T)  1.34 us

profile of v5, /device:TPU:1, one launch (start us, length us, event | category | flops | bytes accessed | tf_op | source)
XLA Modules:
  0.0 57.2 jit_solution(6687775122062516695)
XLA Ops:
  0.6 55.2 %shard_map.76 = f32[24,256]{1,0:T(8,128)} custom-call(f32[32,256]{1,0:T(8,128)} %bitcast.11, f32[1,32]{1,0:T(1,128)} %bitcast.15, f32[8,256]{1,0:T(8,128)} %bitcast.12, f32[8,256]{1,0:T(8,128)} %bitcast.13, f32[8,256]{1,0:T(8,128)} %bitcast.14), custom_call_target="tpu_custom_call" | custom-call | flops 20000000000 | bytes 1000000 | tf_op jit(solution)/shard_map/pallas_call | solution.py:413
  55.9 1.3 %slice_bitcast_fusion = (f32[256,8]{0,1:T(8,128)}, f32[256,8]{0,1:T(8,128)}, f32[256,8]{0,1:T(8,128)}) fusion(f32[24,256]{1,0:T(8,128)} %shard_map.76), kind=kLoop, calls=%fused_computation | loop fusion | bytes 49152 | tf_op jit(solution)/shard_map/transpose | solution.py:447

commit v6 on v5

--- a/solution.py
+++ b/solution.py
@@ -214,8 +214,7 @@
     ]
     for copy in loads:
         copy.start()
-    sums_b[...] = jnp.zeros_like(sums_b)
-    for copy in loads:
+    for copy in loads[:3]:
         copy.wait()
 
     lengths = jnp.transpose(jnp.broadcast_to(inv_ref[...], (DIM, DIM)))[:, :1]
@@ -239,6 +238,9 @@
         vals_b[:, at] = two_pieces(block[DIM:PACK, :]).astype(H)
         eighth_b[:, at] = two_eighths(block[DIM:PACK, :]).astype(Q)
 
+    sums_b[...] = jnp.zeros_like(sums_b)
+    for copy in loads[3:]:
+        copy.wait()
     prepare_b(0, pack[...])
 
     def arrive_b(o, carry):
@@ -341,6 +343,10 @@
     fine = product(eighth_b[...], low)
     image = image + (out[:RHS] + out[RHS:] + (fine[:RHS] + fine[RHS:2 * RHS]))
 
+    direction = dir_ref[...]
+    residual = res_ref[...]
+    old_pair = dot_pair(residual, residual)
+
     for i in range(len(every)):
         copy = remote(send_a.at[i], back_a.at[i], ra_send.at[i], ra_recv.at[i], row_shift(1))
         copy.wait_recv()
@@ -349,12 +355,10 @@
         remote(send_b.at[o], back_b.at[o], rb_send.at[o], rb_recv.at[o], row_shift(1)).wait_recv()
         image = image + back_b[o]
 
-    direction = dir_ref[...]
-    residual = res_ref[...]
     image = GAIN * image + noise_level * direction
 
     lane = lax.broadcasted_iota(jnp.int32, (RHS, 128), 1)
-    pairs = [dot_pair(residual, residual), dot_pair(direction, image), dot_pair(residual, image), dot_pair(image, image)]
+    pairs = [old_pair, dot_pair(direction, image), dot_pair(residual, image), dot_pair(image, image)]
     mixed = jnp.zeros((RHS, 128), F)
     for q, pair in enumerate(pairs):
         mixed = jnp.where(lane == q, pair[0], jnp.where(lane == q + 4, pair[1], mixed))

time: 57.4 us -> 57.4 us (level)
  no operation moved by 1% of the time
where the time goes in v6:
time: 57.4 us; the launch traced here: 57.2 us
  Pallas kernels  55.2 us (96%)
  local copies, waits for them, and re-layouts  1.34 us (2%)
  between operations  0.64 us (1%)
    pallas_call x1, Pallas kernels, local(): pl.pallas_call(functools.partial(kernel, (nr, nz, ny, whole, half)), out_...  55.2 us
    transpose x1, local copies, waits for them, and re-layouts, local(): return (flat[0:8].T, flat[8:16].T, flat[16:24].T)  1.34 us

profile of v6, /device:TPU:1, one launch (start us, length us, event | category | flops | bytes accessed | tf_op | source)
XLA Modules:
  0.0 57.2 jit_solution(12437056370339937083)
XLA Ops:
  0.6 55.2 %shard_map.76 = f32[24,256]{1,0:T(8,128)} custom-call(f32[32,256]{1,0:T(8,128)} %bitcast.11, f32[1,32]{1,0:T(1,128)} %bitcast.15, f32[8,256]{1,0:T(8,128)} %bitcast.12, f32[8,256]{1,0:T(8,128)} %bitcast.13, f32[8,256]{1,0:T(8,128)} %bitcast.14), custom_call_target="tpu_custom_call" | custom-call | flops 20000000000 | bytes 1000000 | tf_op jit(solution)/shard_map/pallas_call | solution.py:417
  55.9 1.3 %slice_bitcast_fusion = (f32[256,8]{0,1:T(8,128)}, f32[256,8]{0,1:T(8,128)}, f32[256,8]{0,1:T(8,128)}) fusion(f32[24,256]{1,0:T(8,128)} %shard_map.76), kind=kLoop, calls=%fused_computation | loop fusion | bytes 49152 | tf_op jit(solution)/shard_map/transpose | solution.py:451
